TPU v7x, 32 devices: a whole 2x2x4 slice. The times are simulated.
32 devices in a mesh: groups: 2 (over x), seg: 4 (over z), blk: 4 (over y, core).
Axes of the slice: x: 2, y: 2, z: 4, core: 2. Of those that a mesh axis runs over, the one named last changes fastest.
Arguments:
- base_state: float32 [16, 20, 32, 128], P(('groups', 'seg'), None, 'blk'), parts along dimension 0, may hold values from -6 to 6
- direction: float32 [16, 20, 32, 128], P(('groups', 'seg'), None, 'blk'), parts along dimension 0, may hold values from -6 to 6
- coupling: float32 [40, 20], P('groups'), parts along dimension 0, may hold values from -1.25 to 1.25
- tiles: bfloat16 [8, 32, 16, 128, 128], P('seg', 'blk'), may hold values from -0.15625 to 0.15625
- columns: int32 [8, 32, 16], P('seg', 'blk'), may hold values from 0 to 31, as said below
- wet: int32 [32, 128], P('blk'), may hold values 0 or 1
- basis: float32 [8, 16, 20, 32, 128], P(None, ('groups', 'seg'), None, 'blk'), parts along dimension 1, may hold values from -0.0078125 to 0.0078125
Outputs:
- orthogonal: float32 [16, 20, 32, 128], P(('groups', 'seg'), None, 'blk'), parts along dimension 0
- coefficients: float32 [18], P('groups'), parts along dimension 0
There are 2 independent parts, one for each index of `groups`. A program takes and returns all parts, laid end to end along the dimension named above; an argument that names none is the same for every part. Nothing has to cross between parts.
Inputs may be any that keep to these rules, and one draw needn't show every extreme that they name: columns[s, r, k] = (r + d) mod 32 for some whole d with -2 <= d <= 2; in every segment some entry has d = 2 and some has d = -2.
All inputs are finite; a program needn't handle non-finite values. No bound on the sum of `wet` on one device may be relied on, other than what follows from the above.
Results may differ from a plain program's by a relative error of at most 0.04.
Values may be sent and summed in bfloat16 or wider, within the bound.
A program may use at most 128 MiB of HBM per device.

v0:
```python
import jax
import jax.numpy as jnp
from jax import lax
from jax.sharding import PartitionSpec as P

STEPS = 18


def with_halo(cells, sides, width):
    for axis, dim in sides:
        count = lax.axis_size(axis)
        head = lax.slice_in_dim(cells, 0, width, axis=dim)
        tail = lax.slice_in_dim(cells, cells.shape[dim] - width, cells.shape[dim], axis=dim)
        cells = jnp.concatenate(
            [
                lax.ppermute(tail, axis, [(i, (i + 1) % count) for i in range(count)]),
                cells,
                lax.ppermute(head, axis, [((i + 1) % count, i) for i in range(count)]),
            ],
            axis=dim,
        )
    return cells


def shifted(block, axis, distance):
    devices = range(lax.axis_size(axis))
    route = [((i - distance) % len(devices), i) for i in devices]
    return lax.ppermute(block, axis, route)


def pick_blocks(whole, cols_s):
    return jnp.take(whole, cols_s.reshape(-1), axis=1)


def transport(extended, places, tiles_part):
    seg_here = extended.shape[0]
    tracers = extended.shape[1]
    points = extended.shape[3]
    rows = places.shape[1]
    stored = places.shape[2]
    picked = jax.vmap(pick_blocks)(extended, places)
    picked = picked.reshape(seg_here, tracers, rows, stored, points)
    return jnp.einsum("srkpq,strkq->strp", tiles_part, picked, preferred_element_type=jnp.float32)


def forcing(u, slope, coupling):
    source = jnp.einsum("tu,sunp->stnp", coupling, slope * u, precision=lax.Precision.HIGHEST)
    return (u + 0.5 * source).astype(jnp.bfloat16)


def on_device(base_state, direction, coupling, tiles, columns, wet, basis):
    seg_here = direction.shape[0]
    tracers = direction.shape[1]
    blocks = direction.shape[2]
    points = direction.shape[3]
    reach = max(1, blocks // 4)
    total = blocks * lax.axis_size("blk")
    entries = float(seg_here * lax.axis_size("seg") * tracers * total * points)
    first = lax.axis_index("blk") * blocks
    slope = 1.0 - jnp.tanh(base_state) ** 2
    wetf = wet.astype(jnp.float32)
    near = (columns - first + reach) % total

    def single(index, u):
        drive = forcing(u, slope, coupling)
        extended = with_halo(drive, (("blk", 2),), reach)
        return transport(extended, near, tiles) * wetf

    final = lax.fori_loop(0, STEPS, single, direction)
    after = shifted(direction[0:1], "seg", -1)
    following = jnp.concatenate([direction[1:], after], axis=0)
    shot = final - following
    local_proj = jnp.einsum("jstnp,stnp->j", basis, shot, precision=lax.Precision.HIGHEST)
    proj = lax.psum(local_proj, ("seg", "blk"))
    orthogonal = shot - jnp.einsum("j,jstnp->stnp", proj, basis, precision=lax.Precision.HIGHEST)
    squared = lax.psum(jnp.sum(orthogonal * orthogonal), ("seg", "blk"))
    length = jnp.sqrt(squared / entries)
    return (orthogonal, jnp.concatenate([proj, length[None]]))


def solution(mesh):
    in_specs = (
        P(("groups", "seg"), None, "blk", None),
        P(("groups", "seg"), None, "blk", None),
        P("groups", None),
        P("seg", "blk", None, None, None),
        P("seg", "blk", None),
        P("blk", None),
        P(None, ("groups", "seg"), None, "blk", None),
    )
    out_specs = (P(("groups", "seg"), None, "blk", None), P("groups"))
    return jax.shard_map(
        on_device, mesh=mesh, in_specs=in_specs, out_specs=out_specs, check_vma=False
    )
```

profile of v0, /device:TPU:0, one launch (start us, length us, event | category | flops | bytes accessed | tf_op | source)
XLA Modules:
  0.0 270.3 jit_solution(12659576681942761652)
XLA Ops:
  2.3 5.0 %collective-permute-start.2 = (f32[1,20,8,128]{3,2,1,0:T(8,128)}, f32[1,20,8,128]{3,2,1,0:T(8,128)}, u32[]{:S(2)}, u32[]{:S(2)}) collective-permute-start(f32[1,20,8,128]{3,2,1,0:T(8,128)} %get-tuple-element.66), channel_id=1, source_target_pairs={{4,0},{8,4},{12,8},{0,12},{5,1},{9,5},{13,9},{1,13},{6,2},{10,6},{... | collective-permute-start | bytes 245768 | tf_op jit(solution)/shard_map/ppermute | solution.py:28
  10.8 190.2 %while.11 = (s32[]{:T(128)}, f32[2,20,8,128]{3,1,2,0:T(8,128)S(1)}, s32[2,8,16]{2,1,0:T(8,128)S(1)}, f32[2,20,8,128]{3,1,2,0:T(8,128)S(1)}, f32[20,20]{1,0:T(8,1...) while((s32[]{:T(128)}, f32[2,20,8,128]{3,1,2,0:T(8,128)S(1)}, ...), condition=%wide.wide.region_1.2_spmd, body=%wide.wide.region_0.1_spmd.sunk | while | flops 178589184 | bytes 13397229 | solution.py:69
  17.2 4.7 %fusion.64 = f32[2,20,8,128]{3,1,2,0:T(8,128)S(1)} fusion(bf16[2,8,16,128,128]{4,3,2,1,0:T(8,128)(2,1)} %get-tuple-element.173, bf16[2,20,8,16,128]{4,1,3,2,0:T(8,128)(2,1)S(1)} %bitcast.63, pred[2,8,16]{2,1,0:T(8,128)(4,1)S(1)} %compare_and_fusion.3, f32[8,128]{1,0:T(8,128)S(1)} %get-tuple-element.174), kind=kOutput, calls=%fused_computation.9.clone.clone.1 | convolution fusion | flops 168468480 | bytes 9867520 | tf_op jit(solution)/shard_map/while/body/eval_jaxpr/srkpq,strkq->strp/dot_general | solution.py:43
  27.7 4.7 %fusion.64 = f32[2,20,8,128]{3,1,2,0:T(8,128)S(1)} fusion(bf16[2,8,16,128,128]{4,3,2,1,0:T(8,128)(2,1)} %get-tuple-element.173, bf16[2,20,8,16,128]{4,1,3,2,0:T(8,128)(2,1)S(1)} %bitcast.63, pred[2,8,16]{2,1,0:T(8,128)(4,1)S(1)} %compare_and_fusion.3, f32[8,128]{1,0:T(8,128)S(1)} %get-tuple-element.174), kind=kOutput, calls=%fused_computation.9.clone.clone.1 | convolution fusion | flops 168468480 | bytes 9867520 | tf_op jit(solution)/shard_map/while/body/eval_jaxpr/srkpq,strkq->strp/dot_general | solution.py:43
  38.2 4.7 %fusion.64 = f32[2,20,8,128]{3,1,2,0:T(8,128)S(1)} fusion(bf16[2,8,16,128,128]{4,3,2,1,0:T(8,128)(2,1)} %get-tuple-element.173, bf16[2,20,8,16,128]{4,1,3,2,0:T(8,128)(2,1)S(1)} %bitcast.63, pred[2,8,16]{2,1,0:T(8,128)(4,1)S(1)} %compare_and_fusion.3, f32[8,128]{1,0:T(8,128)S(1)} %get-tuple-element.174), kind=kOutput, calls=%fused_computation.9.clone.clone.1 | convolution fusion | flops 168468480 | bytes 9867520 | tf_op jit(solution)/shard_map/while/body/eval_jaxpr/srkpq,strkq->strp/dot_general | solution.py:43
  48.8 4.7 %fusion.64 = f32[2,20,8,128]{3,1,2,0:T(8,128)S(1)} fusion(bf16[2,8,16,128,128]{4,3,2,1,0:T(8,128)(2,1)} %get-tuple-element.173, bf16[2,20,8,16,128]{4,1,3,2,0:T(8,128)(2,1)S(1)} %bitcast.63, pred[2,8,16]{2,1,0:T(8,128)(4,1)S(1)} %compare_and_fusion.3, f32[8,128]{1,0:T(8,128)S(1)} %get-tuple-element.174), kind=kOutput, calls=%fused_computation.9.clone.clone.1 | convolution fusion | flops 168468480 | bytes 9867520 | tf_op jit(solution)/shard_map/while/body/eval_jaxpr/srkpq,strkq->strp/dot_general | solution.py:43
  59.3 4.7 %fusion.64 = f32[2,20,8,128]{3,1,2,0:T(8,128)S(1)} fusion(bf16[2,8,16,128,128]{4,3,2,1,0:T(8,128)(2,1)} %get-tuple-element.173, bf16[2,20,8,16,128]{4,1,3,2,0:T(8,128)(2,1)S(1)} %bitcast.63, pred[2,8,16]{2,1,0:T(8,128)(4,1)S(1)} %compare_and_fusion.3, f32[8,128]{1,0:T(8,128)S(1)} %get-tuple-element.174), kind=kOutput, calls=%fused_computation.9.clone.clone.1 | convolution fusion | flops 168468480 | bytes 9867520 | tf_op jit(solution)/shard_map/while/body/eval_jaxpr/srkpq,strkq->strp/dot_general | solution.py:43
  69.8 4.7 %fusion.64 = f32[2,20,8,128]{3,1,2,0:T(8,128)S(1)} fusion(bf16[2,8,16,128,128]{4,3,2,1,0:T(8,128)(2,1)} %get-tuple-element.173, bf16[2,20,8,16,128]{4,1,3,2,0:T(8,128)(2,1)S(1)} %bitcast.63, pred[2,8,16]{2,1,0:T(8,128)(4,1)S(1)} %compare_and_fusion.3, f32[8,128]{1,0:T(8,128)S(1)} %get-tuple-element.174), kind=kOutput, calls=%fused_computation.9.clone.clone.1 | convolution fusion | flops 168468480 | bytes 9867520 | tf_op jit(solution)/shard_map/while/body/eval_jaxpr/srkpq,strkq->strp/dot_general | solution.py:43
  80.4 4.7 %fusion.64 = f32[2,20,8,128]{3,1,2,0:T(8,128)S(1)} fusion(bf16[2,8,16,128,128]{4,3,2,1,0:T(8,128)(2,1)} %get-tuple-element.173, bf16[2,20,8,16,128]{4,1,3,2,0:T(8,128)(2,1)S(1)} %bitcast.63, pred[2,8,16]{2,1,0:T(8,128)(4,1)S(1)} %compare_and_fusion.3, f32[8,128]{1,0:T(8,128)S(1)} %get-tuple-element.174), kind=kOutput, calls=%fused_computation.9.clone.clone.1 | convolution fusion | flops 168468480 | bytes 9867520 | tf_op jit(solution)/shard_map/while/body/eval_jaxpr/srkpq,strkq->strp/dot_general | solution.py:43
  90.9 4.7 %fusion.64 = f32[2,20,8,128]{3,1,2,0:T(8,128)S(1)} fusion(bf16[2,8,16,128,128]{4,3,2,1,0:T(8,128)(2,1)} %get-tuple-element.173, bf16[2,20,8,16,128]{4,1,3,2,0:T(8,128)(2,1)S(1)} %bitcast.63, pred[2,8,16]{2,1,0:T(8,128)(4,1)S(1)} %compare_and_fusion.3, f32[8,128]{1,0:T(8,128)S(1)} %get-tuple-element.174), kind=kOutput, calls=%fused_computation.9.clone.clone.1 | convolution fusion | flops 168468480 | bytes 9867520 | tf_op jit(solution)/shard_map/while/body/eval_jaxpr/srkpq,strkq->strp/dot_general | solution.py:43
  101.4 4.7 %fusion.64 = f32[2,20,8,128]{3,1,2,0:T(8,128)S(1)} fusion(bf16[2,8,16,128,128]{4,3,2,1,0:T(8,128)(2,1)} %get-tuple-element.173, bf16[2,20,8,16,128]{4,1,3,2,0:T(8,128)(2,1)S(1)} %bitcast.63, pred[2,8,16]{2,1,0:T(8,128)(4,1)S(1)} %compare_and_fusion.3, f32[8,128]{1,0:T(8,128)S(1)} %get-tuple-element.174), kind=kOutput, calls=%fused_computation.9.clone.clone.1 | convolution fusion | flops 168468480 | bytes 9867520 | tf_op jit(solution)/shard_map/while/body/eval_jaxpr/srkpq,strkq->strp/dot_general | solution.py:43
  112.0 4.7 %fusion.64 = f32[2,20,8,128]{3,1,2,0:T(8,128)S(1)} fusion(bf16[2,8,16,128,128]{4,3,2,1,0:T(8,128)(2,1)} %get-tuple-element.173, bf16[2,20,8,16,128]{4,1,3,2,0:T(8,128)(2,1)S(1)} %bitcast.63, pred[2,8,16]{2,1,0:T(8,128)(4,1)S(1)} %compare_and_fusion.3, f32[8,128]{1,0:T(8,128)S(1)} %get-tuple-element.174), kind=kOutput, calls=%fused_computation.9.clone.clone.1 | convolution fusion | flops 168468480 | bytes 9867520 | tf_op jit(solution)/shard_map/while/body/eval_jaxpr/srkpq,strkq->strp/dot_general | solution.py:43
  122.5 4.7 %fusion.64 = f32[2,20,8,128]{3,1,2,0:T(8,128)S(1)} fusion(bf16[2,8,16,128,128]{4,3,2,1,0:T(8,128)(2,1)} %get-tuple-element.173, bf16[2,20,8,16,128]{4,1,3,2,0:T(8,128)(2,1)S(1)} %bitcast.63, pred[2,8,16]{2,1,0:T(8,128)(4,1)S(1)} %compare_and_fusion.3, f32[8,128]{1,0:T(8,128)S(1)} %get-tuple-element.174), kind=kOutput, calls=%fused_computation.9.clone.clone.1 | convolution fusion | flops 168468480 | bytes 9867520 | tf_op jit(solution)/shard_map/while/body/eval_jaxpr/srkpq,strkq->strp/dot_general | solution.py:43
  133.0 4.7 %fusion.64 = f32[2,20,8,128]{3,1,2,0:T(8,128)S(1)} fusion(bf16[2,8,16,128,128]{4,3,2,1,0:T(8,128)(2,1)} %get-tuple-element.173, bf16[2,20,8,16,128]{4,1,3,2,0:T(8,128)(2,1)S(1)} %bitcast.63, pred[2,8,16]{2,1,0:T(8,128)(4,1)S(1)} %compare_and_fusion.3, f32[8,128]{1,0:T(8,128)S(1)} %get-tuple-element.174), kind=kOutput, calls=%fused_computation.9.clone.clone.1 | convolution fusion | flops 168468480 | bytes 9867520 | tf_op jit(solution)/shard_map/while/body/eval_jaxpr/srkpq,strkq->strp/dot_general | solution.py:43
  143.6 4.7 %fusion.64 = f32[2,20,8,128]{3,1,2,0:T(8,128)S(1)} fusion(bf16[2,8,16,128,128]{4,3,2,1,0:T(8,128)(2,1)} %get-tuple-element.173, bf16[2,20,8,16,128]{4,1,3,2,0:T(8,128)(2,1)S(1)} %bitcast.63, pred[2,8,16]{2,1,0:T(8,128)(4,1)S(1)} %compare_and_fusion.3, f32[8,128]{1,0:T(8,128)S(1)} %get-tuple-element.174), kind=kOutput, calls=%fused_computation.9.clone.clone.1 | convolution fusion | flops 168468480 | bytes 9867520 | tf_op jit(solution)/shard_map/while/body/eval_jaxpr/srkpq,strkq->strp/dot_general | solution.py:43
  154.1 4.7 %fusion.64 = f32[2,20,8,128]{3,1,2,0:T(8,128)S(1)} fusion(bf16[2,8,16,128,128]{4,3,2,1,0:T(8,128)(2,1)} %get-tuple-element.173, bf16[2,20,8,16,128]{4,1,3,2,0:T(8,128)(2,1)S(1)} %bitcast.63, pred[2,8,16]{2,1,0:T(8,128)(4,1)S(1)} %compare_and_fusion.3, f32[8,128]{1,0:T(8,128)S(1)} %get-tuple-element.174), kind=kOutput, calls=%fused_computation.9.clone.clone.1 | convolution fusion | flops 168468480 | bytes 9867520 | tf_op jit(solution)/shard_map/while/body/eval_jaxpr/srkpq,strkq->strp/dot_general | solution.py:43
  164.7 4.7 %fusion.64 = f32[2,20,8,128]{3,1,2,0:T(8,128)S(1)} fusion(bf16[2,8,16,128,128]{4,3,2,1,0:T(8,128)(2,1)} %get-tuple-element.173, bf16[2,20,8,16,128]{4,1,3,2,0:T(8,128)(2,1)S(1)} %bitcast.63, pred[2,8,16]{2,1,0:T(8,128)(4,1)S(1)} %compare_and_fusion.3, f32[8,128]{1,0:T(8,128)S(1)} %get-tuple-element.174), kind=kOutput, calls=%fused_computation.9.clone.clone.1 | convolution fusion | flops 168468480 | bytes 9867520 | tf_op jit(solution)/shard_map/while/body/eval_jaxpr/srkpq,strkq->strp/dot_general | solution.py:43
  175.2 4.7 %fusion.64 = f32[2,20,8,128]{3,1,2,0:T(8,128)S(1)} fusion(bf16[2,8,16,128,128]{4,3,2,1,0:T(8,128)(2,1)} %get-tuple-element.173, bf16[2,20,8,16,128]{4,1,3,2,0:T(8,128)(2,1)S(1)} %bitcast.63, pred[2,8,16]{2,1,0:T(8,128)(4,1)S(1)} %compare_and_fusion.3, f32[8,128]{1,0:T(8,128)S(1)} %get-tuple-element.174), kind=kOutput, calls=%fused_computation.9.clone.clone.1 | convolution fusion | flops 168468480 | bytes 9867520 | tf_op jit(solution)/shard_map/while/body/eval_jaxpr/srkpq,strkq->strp/dot_general | solution.py:43
  185.7 4.7 %fusion.64 = f32[2,20,8,128]{3,1,2,0:T(8,128)S(1)} fusion(bf16[2,8,16,128,128]{4,3,2,1,0:T(8,128)(2,1)} %get-tuple-element.173, bf16[2,20,8,16,128]{4,1,3,2,0:T(8,128)(2,1)S(1)} %bitcast.63, pred[2,8,16]{2,1,0:T(8,128)(4,1)S(1)} %compare_and_fusion.3, f32[8,128]{1,0:T(8,128)S(1)} %get-tuple-element.174), kind=kOutput, calls=%fused_computation.9.clone.clone.1 | convolution fusion | flops 168468480 | bytes 9867520 | tf_op jit(solution)/shard_map/while/body/eval_jaxpr/srkpq,strkq->strp/dot_general | solution.py:43
  196.3 4.7 %fusion.64 = f32[2,20,8,128]{3,1,2,0:T(8,128)S(1)} fusion(bf16[2,8,16,128,128]{4,3,2,1,0:T(8,128)(2,1)} %get-tuple-element.173, bf16[2,20,8,16,128]{4,1,3,2,0:T(8,128)(2,1)S(1)} %bitcast.63, pred[2,8,16]{2,1,0:T(8,128)(4,1)S(1)} %compare_and_fusion.3, f32[8,128]{1,0:T(8,128)S(1)} %get-tuple-element.174), kind=kOutput, calls=%fused_computation.9.clone.clone.1 | convolution fusion | flops 168468480 | bytes 9867520 | tf_op jit(solution)/shard_map/while/body/eval_jaxpr/srkpq,strkq->strp/dot_general | solution.py:43
  202.0 3.4 %fusion.27 = f32[8]{0:T(128)S(1)} fusion(f32[8,2,20,8,128]{4,3,2,1,0:T(8,128)S(1)} %copy-done, f32[2,20,8,128,1]{3,2,1,0,4:T(8,128)S(1)} %fusion.34), kind=kOutput, calls=%fused_computation.27 | convolution fusion | flops 3932160 | bytes 1474592 | tf_op jit(solution)/shard_map/jstnp,stnp->j/dot_general | solution.py:73
  205.4 29.5 %psum.14 = f32[8]{0:T(128)S(1)} all-reduce(f32[8]{0:T(128)S(1)} %fusion.27), channel_id=1, replica_groups=mesh['groups'=2,'seg'=4,'blk'=4] {'seg','blk'}, use_global_device_ids=true, to_apply=%region_2.3 | all-reduce | flops 8 | bytes 64 | tf_op jit(solution)/shard_map/psum | solution.py:74
  236.7 2.2 multiply_reduce_fusion
  238.9 30.1 %psum.15 = f32[]{:T(128)} all-reduce(f32[]{:T(128)} %get-tuple-element.61), channel_id=1, replica_groups=mesh['groups'=2,'seg'=4,'blk'=4] {'seg','blk'}, use_global_device_ids=true, to_apply=%region_4.5 | all-reduce | flops 1 | bytes 8 | tf_op jit(solution)/shard_map/psum | solution.py:76
  (192 shorter events, 112.7 us)
Async XLA Ops:
  2.3 198.7 %collective-permute-start.2 = (f32[1,20,8,128]{3,2,1,0:T(8,128)}, f32[1,20,8,128]{3,2,1,0:T(8,128)}, u32[]{:S(2)}, u32[]{:S(2)}) collective-permute-start(f32[1,20,8,128]{3,2,1,0:T(8,128)} %get-tuple-element.66), channel_id=1, source_target_pairs={{4,0},{8,4},{12,8},{0,12},{5,1},{9,5},{13,9},{1,13},{6,2},{10,6},{... | collective-permute-start | bytes 245768 | tf_op jit(solution)/shard_map/ppermute | solution.py:28
  11.8 2.3 collective-permute-start
  12.6 3.3 %collective-permute-start.1 = (bf16[2,20,2,128]{3,1,2,0:T(8,128)(2,1)S(1)}, bf16[2,20,2,128]{3,1,2,0:T(8,128)(2,1)S(1)}, u32[]{:S(2)}, u32[]{:S(2)}) collective-permute-start(bf16[2,20,2,128]{3,1,2,0:T(8,128)(2,1)S(1)} %get-tuple-element.149), channel_id=1, source_target_pairs={{0,1},{1,2},{2,3},{3,0},{4,5},{5,6},{6,7},{7,4},{8,9},{9,10},{10,1... | collective-permute-start | bytes 61448 | tf_op jit(solution)/shard_map/while/body/eval_jaxpr/ppermute | solution.py:16
  23.0 1.6 collective-permute-start
  23.0 3.3 %collective-permute-start.1 = (bf16[2,20,2,128]{3,1,2,0:T(8,128)(2,1)S(1)}, bf16[2,20,2,128]{3,1,2,0:T(8,128)(2,1)S(1)}, u32[]{:S(2)}, u32[]{:S(2)}) collective-permute-start(bf16[2,20,2,128]{3,1,2,0:T(8,128)(2,1)S(1)} %get-tuple-element.149), channel_id=1, source_target_pairs={{0,1},{1,2},{2,3},{3,0},{4,5},{5,6},{6,7},{7,4},{8,9},{9,10},{10,1... | collective-permute-start | bytes 61448 | tf_op jit(solution)/shard_map/while/body/eval_jaxpr/ppermute | solution.py:16
  33.5 1.6 collective-permute-start
  33.6 3.3 %collective-permute-start.1 = (bf16[2,20,2,128]{3,1,2,0:T(8,128)(2,1)S(1)}, bf16[2,20,2,128]{3,1,2,0:T(8,128)(2,1)S(1)}, u32[]{:S(2)}, u32[]{:S(2)}) collective-permute-start(bf16[2,20,2,128]{3,1,2,0:T(8,128)(2,1)S(1)} %get-tuple-element.149), channel_id=1, source_target_pairs={{0,1},{1,2},{2,3},{3,0},{4,5},{5,6},{6,7},{7,4},{8,9},{9,10},{10,1... | collective-permute-start | bytes 61448 | tf_op jit(solution)/shard_map/while/body/eval_jaxpr/ppermute | solution.py:16
  44.1 3.3 %collective-permute-start.1 = (bf16[2,20,2,128]{3,1,2,0:T(8,128)(2,1)S(1)}, bf16[2,20,2,128]{3,1,2,0:T(8,128)(2,1)S(1)}, u32[]{:S(2)}, u32[]{:S(2)}) collective-permute-start(bf16[2,20,2,128]{3,1,2,0:T(8,128)(2,1)S(1)} %get-tuple-element.149), channel_id=1, source_target_pairs={{0,1},{1,2},{2,3},{3,0},{4,5},{5,6},{6,7},{7,4},{8,9},{9,10},{10,1... | collective-permute-start | bytes 61448 | tf_op jit(solution)/shard_map/while/body/eval_jaxpr/ppermute | solution.py:16
  54.6 3.3 %collective-permute-start.1 = (bf16[2,20,2,128]{3,1,2,0:T(8,128)(2,1)S(1)}, bf16[2,20,2,128]{3,1,2,0:T(8,128)(2,1)S(1)}, u32[]{:S(2)}, u32[]{:S(2)}) collective-permute-start(bf16[2,20,2,128]{3,1,2,0:T(8,128)(2,1)S(1)} %get-tuple-element.149), channel_id=1, source_target_pairs={{0,1},{1,2},{2,3},{3,0},{4,5},{5,6},{6,7},{7,4},{8,9},{9,10},{10,1... | collective-permute-start | bytes 61448 | tf_op jit(solution)/shard_map/while/body/eval_jaxpr/ppermute | solution.py:16
  65.2 3.3 %collective-permute-start.1 = (bf16[2,20,2,128]{3,1,2,0:T(8,128)(2,1)S(1)}, bf16[2,20,2,128]{3,1,2,0:T(8,128)(2,1)S(1)}, u32[]{:S(2)}, u32[]{:S(2)}) collective-permute-start(bf16[2,20,2,128]{3,1,2,0:T(8,128)(2,1)S(1)} %get-tuple-element.149), channel_id=1, source_target_pairs={{0,1},{1,2},{2,3},{3,0},{4,5},{5,6},{6,7},{7,4},{8,9},{9,10},{10,1... | collective-permute-start | bytes 61448 | tf_op jit(solution)/shard_map/while/body/eval_jaxpr/ppermute | solution.py:16
  75.7 3.3 %collective-permute-start.1 = (bf16[2,20,2,128]{3,1,2,0:T(8,128)(2,1)S(1)}, bf16[2,20,2,128]{3,1,2,0:T(8,128)(2,1)S(1)}, u32[]{:S(2)}, u32[]{:S(2)}) collective-permute-start(bf16[2,20,2,128]{3,1,2,0:T(8,128)(2,1)S(1)} %get-tuple-element.149), channel_id=1, source_target_pairs={{0,1},{1,2},{2,3},{3,0},{4,5},{5,6},{6,7},{7,4},{8,9},{9,10},{10,1... | collective-permute-start | bytes 61448 | tf_op jit(solution)/shard_map/while/body/eval_jaxpr/ppermute | solution.py:16
  86.2 1.6 collective-permute-start
  86.2 3.3 %collective-permute-start.1 = (bf16[2,20,2,128]{3,1,2,0:T(8,128)(2,1)S(1)}, bf16[2,20,2,128]{3,1,2,0:T(8,128)(2,1)S(1)}, u32[]{:S(2)}, u32[]{:S(2)}) collective-permute-start(bf16[2,20,2,128]{3,1,2,0:T(8,128)(2,1)S(1)} %get-tuple-element.149), channel_id=1, source_target_pairs={{0,1},{1,2},{2,3},{3,0},{4,5},{5,6},{6,7},{7,4},{8,9},{9,10},{10,1... | collective-permute-start | bytes 61448 | tf_op jit(solution)/shard_map/while/body/eval_jaxpr/ppermute | solution.py:16
  96.7 1.6 collective-permute-start
  96.8 3.3 %collective-permute-start.1 = (bf16[2,20,2,128]{3,1,2,0:T(8,128)(2,1)S(1)}, bf16[2,20,2,128]{3,1,2,0:T(8,128)(2,1)S(1)}, u32[]{:S(2)}, u32[]{:S(2)}) collective-permute-start(bf16[2,20,2,128]{3,1,2,0:T(8,128)(2,1)S(1)} %get-tuple-element.149), channel_id=1, source_target_pairs={{0,1},{1,2},{2,3},{3,0},{4,5},{5,6},{6,7},{7,4},{8,9},{9,10},{10,1... | collective-permute-start | bytes 61448 | tf_op jit(solution)/shard_map/while/body/eval_jaxpr/ppermute | solution.py:16
  107.3 3.3 %collective-permute-start.1 = (bf16[2,20,2,128]{3,1,2,0:T(8,128)(2,1)S(1)}, bf16[2,20,2,128]{3,1,2,0:T(8,128)(2,1)S(1)}, u32[]{:S(2)}, u32[]{:S(2)}) collective-permute-start(bf16[2,20,2,128]{3,1,2,0:T(8,128)(2,1)S(1)} %get-tuple-element.149), channel_id=1, source_target_pairs={{0,1},{1,2},{2,3},{3,0},{4,5},{5,6},{6,7},{7,4},{8,9},{9,10},{10,1... | collective-permute-start | bytes 61448 | tf_op jit(solution)/shard_map/while/body/eval_jaxpr/ppermute | solution.py:16
  117.8 3.3 %collective-permute-start.1 = (bf16[2,20,2,128]{3,1,2,0:T(8,128)(2,1)S(1)}, bf16[2,20,2,128]{3,1,2,0:T(8,128)(2,1)S(1)}, u32[]{:S(2)}, u32[]{:S(2)}) collective-permute-start(bf16[2,20,2,128]{3,1,2,0:T(8,128)(2,1)S(1)} %get-tuple-element.149), channel_id=1, source_target_pairs={{0,1},{1,2},{2,3},{3,0},{4,5},{5,6},{6,7},{7,4},{8,9},{9,10},{10,1... | collective-permute-start | bytes 61448 | tf_op jit(solution)/shard_map/while/body/eval_jaxpr/ppermute | solution.py:16
  128.4 3.3 %collective-permute-start.1 = (bf16[2,20,2,128]{3,1,2,0:T(8,128)(2,1)S(1)}, bf16[2,20,2,128]{3,1,2,0:T(8,128)(2,1)S(1)}, u32[]{:S(2)}, u32[]{:S(2)}) collective-permute-start(bf16[2,20,2,128]{3,1,2,0:T(8,128)(2,1)S(1)} %get-tuple-element.149), channel_id=1, source_target_pairs={{0,1},{1,2},{2,3},{3,0},{4,5},{5,6},{6,7},{7,4},{8,9},{9,10},{10,1... | collective-permute-start | bytes 61448 | tf_op jit(solution)/shard_map/while/body/eval_jaxpr/ppermute | solution.py:16
  138.9 3.3 %collective-permute-start.1 = (bf16[2,20,2,128]{3,1,2,0:T(8,128)(2,1)S(1)}, bf16[2,20,2,128]{3,1,2,0:T(8,128)(2,1)S(1)}, u32[]{:S(2)}, u32[]{:S(2)}) collective-permute-start(bf16[2,20,2,128]{3,1,2,0:T(8,128)(2,1)S(1)} %get-tuple-element.149), channel_id=1, source_target_pairs={{0,1},{1,2},{2,3},{3,0},{4,5},{5,6},{6,7},{7,4},{8,9},{9,10},{10,1... | collective-permute-start | bytes 61448 | tf_op jit(solution)/shard_map/while/body/eval_jaxpr/ppermute | solution.py:16
  149.4 3.3 %collective-permute-start.1 = (bf16[2,20,2,128]{3,1,2,0:T(8,128)(2,1)S(1)}, bf16[2,20,2,128]{3,1,2,0:T(8,128)(2,1)S(1)}, u32[]{:S(2)}, u32[]{:S(2)}) collective-permute-start(bf16[2,20,2,128]{3,1,2,0:T(8,128)(2,1)S(1)} %get-tuple-element.149), channel_id=1, source_target_pairs={{0,1},{1,2},{2,3},{3,0},{4,5},{5,6},{6,7},{7,4},{8,9},{9,10},{10,1... | collective-permute-start | bytes 61448 | tf_op jit(solution)/shard_map/while/body/eval_jaxpr/ppermute | solution.py:16
  160.0 3.3 %collective-permute-start.1 = (bf16[2,20,2,128]{3,1,2,0:T(8,128)(2,1)S(1)}, bf16[2,20,2,128]{3,1,2,0:T(8,128)(2,1)S(1)}, u32[]{:S(2)}, u32[]{:S(2)}) collective-permute-start(bf16[2,20,2,128]{3,1,2,0:T(8,128)(2,1)S(1)} %get-tuple-element.149), channel_id=1, source_target_pairs={{0,1},{1,2},{2,3},{3,0},{4,5},{5,6},{6,7},{7,4},{8,9},{9,10},{10,1... | collective-permute-start | bytes 61448 | tf_op jit(solution)/shard_map/while/body/eval_jaxpr/ppermute | solution.py:16
  170.5 3.3 %collective-permute-start.1 = (bf16[2,20,2,128]{3,1,2,0:T(8,128)(2,1)S(1)}, bf16[2,20,2,128]{3,1,2,0:T(8,128)(2,1)S(1)}, u32[]{:S(2)}, u32[]{:S(2)}) collective-permute-start(bf16[2,20,2,128]{3,1,2,0:T(8,128)(2,1)S(1)} %get-tuple-element.149), channel_id=1, source_target_pairs={{0,1},{1,2},{2,3},{3,0},{4,5},{5,6},{6,7},{7,4},{8,9},{9,10},{10,1... | collective-permute-start | bytes 61448 | tf_op jit(solution)/shard_map/while/body/eval_jaxpr/ppermute | solution.py:16
  181.1 3.3 %collective-permute-start.1 = (bf16[2,20,2,128]{3,1,2,0:T(8,128)(2,1)S(1)}, bf16[2,20,2,128]{3,1,2,0:T(8,128)(2,1)S(1)}, u32[]{:S(2)}, u32[]{:S(2)}) collective-permute-start(bf16[2,20,2,128]{3,1,2,0:T(8,128)(2,1)S(1)} %get-tuple-element.149), channel_id=1, source_target_pairs={{0,1},{1,2},{2,3},{3,0},{4,5},{5,6},{6,7},{7,4},{8,9},{9,10},{10,1... | collective-permute-start | bytes 61448 | tf_op jit(solution)/shard_map/while/body/eval_jaxpr/ppermute | solution.py:16
  191.6 3.3 %collective-permute-start.1 = (bf16[2,20,2,128]{3,1,2,0:T(8,128)(2,1)S(1)}, bf16[2,20,2,128]{3,1,2,0:T(8,128)(2,1)S(1)}, u32[]{:S(2)}, u32[]{:S(2)}) collective-permute-start(bf16[2,20,2,128]{3,1,2,0:T(8,128)(2,1)S(1)} %get-tuple-element.149), channel_id=1, source_target_pairs={{0,1},{1,2},{2,3},{3,0},{4,5},{5,6},{6,7},{7,4},{8,9},{9,10},{10,1... | collective-permute-start | bytes 61448 | tf_op jit(solution)/shard_map/while/body/eval_jaxpr/ppermute | solution.py:16
  (14 other events, 221.8 us)
where the time goes:
time: 272 us; the launch traced here: 270 us
  matrix products  109 us (40%)
  blocking collectives  59.6 us (22%)
  waiting for transfers between devices  50.7 us (19%)
  local copies, waits for them, and re-layouts  26.8 us (10%)
  starting transfers between devices  15.2 us (6%)
  other arithmetic  6.83 us (3%)
    dot_general x18, matrix products, transport(): jnp.einsum('srkpq,strkq->strp', tiles_part, picked, preferred_element_typ...  85.2 us
    ppermute x18, waiting for transfers between devices, with_halo(): lax.ppermute(tail, axis, [(i, (i + 1) % count) for i in range(count)])  32.2 us
    psum x1, blocking collectives, on_device(): squared = lax.psum(jnp.sum(orthogonal * orthogonal), ('seg', 'blk'))  30.1 us
    psum x1, blocking collectives, on_device(): proj = lax.psum(local_proj, ('seg', 'blk'))  29.5 us
    gather x18, local copies, waits for them, and re-layouts, pick_blocks(): return jnp.take(whole, cols_s.reshape(-1), axis=1)  23.9 us
    dot_general x18, matrix products, forcing(): jnp.einsum('tu,sunp->stnp', coupling, slope * u, precision=lax.Precision....  18.7 us
    ppermute x18, waiting for transfers between devices, with_halo(): lax.ppermute(head, axis, [((i + 1) % count, i) for i in range(count)])  18.5 us
    ppermute x18, starting transfers between devices, with_halo(): lax.ppermute(tail, axis, [(i, (i + 1) % count) for i in range(count)])  8.45 us
  transfers between devices with their start and end apart: 37, of which 36 were waited for; matrix products, arithmetic and copies ran while one was open for 49% of the time, Pallas kernels for 0%

commit v1 on v0

--- a/solution.py
+++ b/solution.py
@@ -71,7 +71,7 @@
     following = jnp.concatenate([direction[1:], after], axis=0)
     shot = final - following
     local_proj = jnp.einsum("jstnp,stnp->j", basis, shot, precision=lax.Precision.HIGHEST)
-    proj = lax.psum(local_proj, ("seg", "blk"))
+    proj = lax.psum(lax.psum(local_proj, "blk"), "seg")
     orthogonal = shot - jnp.einsum("j,jstnp->stnp", proj, basis, precision=lax.Precision.HIGHEST)
     squared = lax.psum(jnp.sum(orthogonal * orthogonal), ("seg", "blk"))
     length = jnp.sqrt(squared / entries)

time: 272 us -> 257 us (0.945)
  blocking collectives: 59.6 us -> 44.6 us
    psum x1 -> x2, blocking collectives: 29.5 us -> 14.5 us  [on_device(): proj = lax.psum(lax.psum(local_proj, 'blk'), 'seg')]
  transfers between devices with their start and end apart: 37 -> 37, of which waited for: 36 -> 36; matrix products, arithmetic and copies ran while one was open for 49% -> 52% of each run, Pallas kernels for 0% -> 0%
where the time goes in v1:
time: 257 us; the launch traced here: 255 us
  matrix products  109 us (42%)
  waiting for transfers between devices  50.7 us (20%)
  blocking collectives  44.6 us (17%)
  local copies, waits for them, and re-layouts  26.8 us (10%)
  starting transfers between devices  15.2 us (6%)
  other arithmetic  6.83 us (3%)
    dot_general x18, matrix products, transport(): jnp.einsum('srkpq,strkq->strp', tiles_part, picked, preferred_element_typ...  85.2 us
    ppermute x18, waiting for transfers between devices, with_halo(): lax.ppermute(tail, axis, [(i, (i + 1) % count) for i in range(count)])  32.2 us
    psum x1, blocking collectives, on_device(): squared = lax.psum(jnp.sum(orthogonal * orthogonal), ('seg', 'blk'))  30.1 us
    gather x18, local copies, waits for them, and re-layouts, pick_blocks(): return jnp.take(whole, cols_s.reshape(-1), axis=1)  23.9 us
    dot_general x18, matrix products, forcing(): jnp.einsum('tu,sunp->stnp', coupling, slope * u, precision=lax.Precision....  18.7 us
    ppermute x18, waiting for transfers between devices, with_halo(): lax.ppermute(head, axis, [((i + 1) % count, i) for i in range(count)])  18.5 us
    psum x2, blocking collectives, on_device(): proj = lax.psum(lax.psum(local_proj, 'blk'), 'seg')  14.5 us
    ppermute x18, starting transfers between devices, with_halo(): lax.ppermute(tail, axis, [(i, (i + 1) % count) for i in range(count)])  8.45 us
  transfers between devices with their start and end apart: 37, of which 36 were waited for; matrix products, arithmetic and copies ran while one was open for 52% of the time, Pallas kernels for 0%

profile of v1, /device:TPU:0, one launch (start us, length us, event | category | flops | bytes accessed | tf_op | source)
XLA Modules:
  0.0 255.3 jit_solution(16893796193607019343)
XLA Ops:
  2.3 5.0 %collective-permute-start.2 = (f32[1,20,8,128]{3,2,1,0:T(8,128)}, f32[1,20,8,128]{3,2,1,0:T(8,128)}, u32[]{:S(2)}, u32[]{:S(2)}) collective-permute-start(f32[1,20,8,128]{3,2,1,0:T(8,128)} %get-tuple-element.66), channel_id=1, source_target_pairs={{4,0},{8,4},{12,8},{0,12},{5,1},{9,5},{13,9},{1,13},{6,2},{10,6},{... | collective-permute-start | bytes 245768 | tf_op jit(solution)/shard_map/ppermute | solution.py:28
  10.8 190.2 %while.11 = (s32[]{:T(128)}, f32[2,20,8,128]{3,1,2,0:T(8,128)S(1)}, s32[2,8,16]{2,1,0:T(8,128)S(1)}, f32[2,20,8,128]{3,1,2,0:T(8,128)S(1)}, f32[20,20]{1,0:T(8,1...) while((s32[]{:T(128)}, f32[2,20,8,128]{3,1,2,0:T(8,128)S(1)}, ...), condition=%wide.wide.region_1.2_spmd, body=%wide.wide.region_0.1_spmd.sunk | while | flops 178589184 | bytes 13397229 | solution.py:69
  17.2 4.7 %fusion.64 = f32[2,20,8,128]{3,1,2,0:T(8,128)S(1)} fusion(bf16[2,8,16,128,128]{4,3,2,1,0:T(8,128)(2,1)} %get-tuple-element.173, bf16[2,20,8,16,128]{4,1,3,2,0:T(8,128)(2,1)S(1)} %bitcast.63, pred[2,8,16]{2,1,0:T(8,128)(4,1)S(1)} %compare_and_fusion.3, f32[8,128]{1,0:T(8,128)S(1)} %get-tuple-element.174), kind=kOutput, calls=%fused_computation.9.clone.clone.1 | convolution fusion | flops 168468480 | bytes 9867520 | tf_op jit(solution)/shard_map/while/body/eval_jaxpr/srkpq,strkq->strp/dot_general | solution.py:43
  27.7 4.7 %fusion.64 = f32[2,20,8,128]{3,1,2,0:T(8,128)S(1)} fusion(bf16[2,8,16,128,128]{4,3,2,1,0:T(8,128)(2,1)} %get-tuple-element.173, bf16[2,20,8,16,128]{4,1,3,2,0:T(8,128)(2,1)S(1)} %bitcast.63, pred[2,8,16]{2,1,0:T(8,128)(4,1)S(1)} %compare_and_fusion.3, f32[8,128]{1,0:T(8,128)S(1)} %get-tuple-element.174), kind=kOutput, calls=%fused_computation.9.clone.clone.1 | convolution fusion | flops 168468480 | bytes 9867520 | tf_op jit(solution)/shard_map/while/body/eval_jaxpr/srkpq,strkq->strp/dot_general | solution.py:43
  38.2 4.7 %fusion.64 = f32[2,20,8,128]{3,1,2,0:T(8,128)S(1)} fusion(bf16[2,8,16,128,128]{4,3,2,1,0:T(8,128)(2,1)} %get-tuple-element.173, bf16[2,20,8,16,128]{4,1,3,2,0:T(8,128)(2,1)S(1)} %bitcast.63, pred[2,8,16]{2,1,0:T(8,128)(4,1)S(1)} %compare_and_fusion.3, f32[8,128]{1,0:T(8,128)S(1)} %get-tuple-element.174), kind=kOutput, calls=%fused_computation.9.clone.clone.1 | convolution fusion | flops 168468480 | bytes 9867520 | tf_op jit(solution)/shard_map/while/body/eval_jaxpr/srkpq,strkq->strp/dot_general | solution.py:43
  48.8 4.7 %fusion.64 = f32[2,20,8,128]{3,1,2,0:T(8,128)S(1)} fusion(bf16[2,8,16,128,128]{4,3,2,1,0:T(8,128)(2,1)} %get-tuple-element.173, bf16[2,20,8,16,128]{4,1,3,2,0:T(8,128)(2,1)S(1)} %bitcast.63, pred[2,8,16]{2,1,0:T(8,128)(4,1)S(1)} %compare_and_fusion.3, f32[8,128]{1,0:T(8,128)S(1)} %get-tuple-element.174), kind=kOutput, calls=%fused_computation.9.clone.clone.1 | convolution fusion | flops 168468480 | bytes 9867520 | tf_op jit(solution)/shard_map/while/body/eval_jaxpr/srkpq,strkq->strp/dot_general | solution.py:43
  59.3 4.7 %fusion.64 = f32[2,20,8,128]{3,1,2,0:T(8,128)S(1)} fusion(bf16[2,8,16,128,128]{4,3,2,1,0:T(8,128)(2,1)} %get-tuple-element.173, bf16[2,20,8,16,128]{4,1,3,2,0:T(8,128)(2,1)S(1)} %bitcast.63, pred[2,8,16]{2,1,0:T(8,128)(4,1)S(1)} %compare_and_fusion.3, f32[8,128]{1,0:T(8,128)S(1)} %get-tuple-element.174), kind=kOutput, calls=%fused_computation.9.clone.clone.1 | convolution fusion | flops 168468480 | bytes 9867520 | tf_op jit(solution)/shard_map/while/body/eval_jaxpr/srkpq,strkq->strp/dot_general | solution.py:43
  69.8 4.7 %fusion.64 = f32[2,20,8,128]{3,1,2,0:T(8,128)S(1)} fusion(bf16[2,8,16,128,128]{4,3,2,1,0:T(8,128)(2,1)} %get-tuple-element.173, bf16[2,20,8,16,128]{4,1,3,2,0:T(8,128)(2,1)S(1)} %bitcast.63, pred[2,8,16]{2,1,0:T(8,128)(4,1)S(1)} %compare_and_fusion.3, f32[8,128]{1,0:T(8,128)S(1)} %get-tuple-element.174), kind=kOutput, calls=%fused_computation.9.clone.clone.1 | convolution fusion | flops 168468480 | bytes 9867520 | tf_op jit(solution)/shard_map/while/body/eval_jaxpr/srkpq,strkq->strp/dot_general | solution.py:43
  80.4 4.7 %fusion.64 = f32[2,20,8,128]{3,1,2,0:T(8,128)S(1)} fusion(bf16[2,8,16,128,128]{4,3,2,1,0:T(8,128)(2,1)} %get-tuple-element.173, bf16[2,20,8,16,128]{4,1,3,2,0:T(8,128)(2,1)S(1)} %bitcast.63, pred[2,8,16]{2,1,0:T(8,128)(4,1)S(1)} %compare_and_fusion.3, f32[8,128]{1,0:T(8,128)S(1)} %get-tuple-element.174), kind=kOutput, calls=%fused_computation.9.clone.clone.1 | convolution fusion | flops 168468480 | bytes 9867520 | tf_op jit(solution)/shard_map/while/body/eval_jaxpr/srkpq,strkq->strp/dot_general | solution.py:43
  90.9 4.7 %fusion.64 = f32[2,20,8,128]{3,1,2,0:T(8,128)S(1)} fusion(bf16[2,8,16,128,128]{4,3,2,1,0:T(8,128)(2,1)} %get-tuple-element.173, bf16[2,20,8,16,128]{4,1,3,2,0:T(8,128)(2,1)S(1)} %bitcast.63, pred[2,8,16]{2,1,0:T(8,128)(4,1)S(1)} %compare_and_fusion.3, f32[8,128]{1,0:T(8,128)S(1)} %get-tuple-element.174), kind=kOutput, calls=%fused_computation.9.clone.clone.1 | convolution fusion | flops 168468480 | bytes 9867520 | tf_op jit(solution)/shard_map/while/body/eval_jaxpr/srkpq,strkq->strp/dot_general | solution.py:43
  101.4 4.7 %fusion.64 = f32[2,20,8,128]{3,1,2,0:T(8,128)S(1)} fusion(bf16[2,8,16,128,128]{4,3,2,1,0:T(8,128)(2,1)} %get-tuple-element.173, bf16[2,20,8,16,128]{4,1,3,2,0:T(8,128)(2,1)S(1)} %bitcast.63, pred[2,8,16]{2,1,0:T(8,128)(4,1)S(1)} %compare_and_fusion.3, f32[8,128]{1,0:T(8,128)S(1)} %get-tuple-element.174), kind=kOutput, calls=%fused_computation.9.clone.clone.1 | convolution fusion | flops 168468480 | bytes 9867520 | tf_op jit(solution)/shard_map/while/body/eval_jaxpr/srkpq,strkq->strp/dot_general | solution.py:43
  112.0 4.7 %fusion.64 = f32[2,20,8,128]{3,1,2,0:T(8,128)S(1)} fusion(bf16[2,8,16,128,128]{4,3,2,1,0:T(8,128)(2,1)} %get-tuple-element.173, bf16[2,20,8,16,128]{4,1,3,2,0:T(8,128)(2,1)S(1)} %bitcast.63, pred[2,8,16]{2,1,0:T(8,128)(4,1)S(1)} %compare_and_fusion.3, f32[8,128]{1,0:T(8,128)S(1)} %get-tuple-element.174), kind=kOutput, calls=%fused_computation.9.clone.clone.1 | convolution fusion | flops 168468480 | bytes 9867520 | tf_op jit(solution)/shard_map/while/body/eval_jaxpr/srkpq,strkq->strp/dot_general | solution.py:43
  122.5 4.7 %fusion.64 = f32[2,20,8,128]{3,1,2,0:T(8,128)S(1)} fusion(bf16[2,8,16,128,128]{4,3,2,1,0:T(8,128)(2,1)} %get-tuple-element.173, bf16[2,20,8,16,128]{4,1,3,2,0:T(8,128)(2,1)S(1)} %bitcast.63, pred[2,8,16]{2,1,0:T(8,128)(4,1)S(1)} %compare_and_fusion.3, f32[8,128]{1,0:T(8,128)S(1)} %get-tuple-element.174), kind=kOutput, calls=%fused_computation.9.clone.clone.1 | convolution fusion | flops 168468480 | bytes 9867520 | tf_op jit(solution)/shard_map/while/body/eval_jaxpr/srkpq,strkq->strp/dot_general | solution.py:43
  133.0 4.7 %fusion.64 = f32[2,20,8,128]{3,1,2,0:T(8,128)S(1)} fusion(bf16[2,8,16,128,128]{4,3,2,1,0:T(8,128)(2,1)} %get-tuple-element.173, bf16[2,20,8,16,128]{4,1,3,2,0:T(8,128)(2,1)S(1)} %bitcast.63, pred[2,8,16]{2,1,0:T(8,128)(4,1)S(1)} %compare_and_fusion.3, f32[8,128]{1,0:T(8,128)S(1)} %get-tuple-element.174), kind=kOutput, calls=%fused_computation.9.clone.clone.1 | convolution fusion | flops 168468480 | bytes 9867520 | tf_op jit(solution)/shard_map/while/body/eval_jaxpr/srkpq,strkq->strp/dot_general | solution.py:43
  143.6 4.7 %fusion.64 = f32[2,20,8,128]{3,1,2,0:T(8,128)S(1)} fusion(bf16[2,8,16,128,128]{4,3,2,1,0:T(8,128)(2,1)} %get-tuple-element.173, bf16[2,20,8,16,128]{4,1,3,2,0:T(8,128)(2,1)S(1)} %bitcast.63, pred[2,8,16]{2,1,0:T(8,128)(4,1)S(1)} %compare_and_fusion.3, f32[8,128]{1,0:T(8,128)S(1)} %get-tuple-element.174), kind=kOutput, calls=%fused_computation.9.clone.clone.1 | convolution fusion | flops 168468480 | bytes 9867520 | tf_op jit(solution)/shard_map/while/body/eval_jaxpr/srkpq,strkq->strp/dot_general | solution.py:43
  154.1 4.7 %fusion.64 = f32[2,20,8,128]{3,1,2,0:T(8,128)S(1)} fusion(bf16[2,8,16,128,128]{4,3,2,1,0:T(8,128)(2,1)} %get-tuple-element.173, bf16[2,20,8,16,128]{4,1,3,2,0:T(8,128)(2,1)S(1)} %bitcast.63, pred[2,8,16]{2,1,0:T(8,128)(4,1)S(1)} %compare_and_fusion.3, f32[8,128]{1,0:T(8,128)S(1)} %get-tuple-element.174), kind=kOutput, calls=%fused_computation.9.clone.clone.1 | convolution fusion | flops 168468480 | bytes 9867520 | tf_op jit(solution)/shard_map/while/body/eval_jaxpr/srkpq,strkq->strp/dot_general | solution.py:43
  164.7 4.7 %fusion.64 = f32[2,20,8,128]{3,1,2,0:T(8,128)S(1)} fusion(bf16[2,8,16,128,128]{4,3,2,1,0:T(8,128)(2,1)} %get-tuple-element.173, bf16[2,20,8,16,128]{4,1,3,2,0:T(8,128)(2,1)S(1)} %bitcast.63, pred[2,8,16]{2,1,0:T(8,128)(4,1)S(1)} %compare_and_fusion.3, f32[8,128]{1,0:T(8,128)S(1)} %get-tuple-element.174), kind=kOutput, calls=%fused_computation.9.clone.clone.1 | convolution fusion | flops 168468480 | bytes 9867520 | tf_op jit(solution)/shard_map/while/body/eval_jaxpr/srkpq,strkq->strp/dot_general | solution.py:43
  175.2 4.7 %fusion.64 = f32[2,20,8,128]{3,1,2,0:T(8,128)S(1)} fusion(bf16[2,8,16,128,128]{4,3,2,1,0:T(8,128)(2,1)} %get-tuple-element.173, bf16[2,20,8,16,128]{4,1,3,2,0:T(8,128)(2,1)S(1)} %bitcast.63, pred[2,8,16]{2,1,0:T(8,128)(4,1)S(1)} %compare_and_fusion.3, f32[8,128]{1,0:T(8,128)S(1)} %get-tuple-element.174), kind=kOutput, calls=%fused_computation.9.clone.clone.1 | convolution fusion | flops 168468480 | bytes 9867520 | tf_op jit(solution)/shard_map/while/body/eval_jaxpr/srkpq,strkq->strp/dot_general | solution.py:43
  185.7 4.7 %fusion.64 = f32[2,20,8,128]{3,1,2,0:T(8,128)S(1)} fusion(bf16[2,8,16,128,128]{4,3,2,1,0:T(8,128)(2,1)} %get-tuple-element.173, bf16[2,20,8,16,128]{4,1,3,2,0:T(8,128)(2,1)S(1)} %bitcast.63, pred[2,8,16]{2,1,0:T(8,128)(4,1)S(1)} %compare_and_fusion.3, f32[8,128]{1,0:T(8,128)S(1)} %get-tuple-element.174), kind=kOutput, calls=%fused_computation.9.clone.clone.1 | convolution fusion | flops 168468480 | bytes 9867520 | tf_op jit(solution)/shard_map/while/body/eval_jaxpr/srkpq,strkq->strp/dot_general | solution.py:43
  196.3 4.7 %fusion.64 = f32[2,20,8,128]{3,1,2,0:T(8,128)S(1)} fusion(bf16[2,8,16,128,128]{4,3,2,1,0:T(8,128)(2,1)} %get-tuple-element.173, bf16[2,20,8,16,128]{4,1,3,2,0:T(8,128)(2,1)S(1)} %bitcast.63, pred[2,8,16]{2,1,0:T(8,128)(4,1)S(1)} %compare_and_fusion.3, f32[8,128]{1,0:T(8,128)S(1)} %get-tuple-element.174), kind=kOutput, calls=%fused_computation.9.clone.clone.1 | convolution fusion | flops 168468480 | bytes 9867520 | tf_op jit(solution)/shard_map/while/body/eval_jaxpr/srkpq,strkq->strp/dot_general | solution.py:43
  202.0 3.4 %fusion.27 = f32[8]{0:T(128)S(1)} fusion(f32[8,2,20,8,128]{4,3,2,1,0:T(8,128)S(1)} %copy-done, f32[2,20,8,128,1]{3,2,1,0,4:T(8,128)S(1)} %fusion.34), kind=kOutput, calls=%fused_computation.27 | convolution fusion | flops 3932160 | bytes 1474592 | tf_op jit(solution)/shard_map/jstnp,stnp->j/dot_general | solution.py:73
  205.4 5.7 %psum.21 = f32[8]{0:T(128)S(1)} all-reduce(f32[8]{0:T(128)S(1)} %fusion.27), channel_id=1, replica_groups=mesh['groups'=2,'seg'=4,'blk'=4] {'blk'}, use_global_device_ids=true, to_apply=%region_2.3 | all-reduce | flops 8 | bytes 64 | tf_op jit(solution)/shard_map/psum | solution.py:74
  211.0 8.8 %psum.22 = f32[8]{0:T(128)S(1)} all-reduce(f32[8]{0:T(128)S(1)} %psum.21), channel_id=1, replica_groups=mesh['groups'=2,'seg'=4,'blk'=4] {'seg'}, use_global_device_ids=true, to_apply=%region_3.4 | all-reduce | flops 8 | bytes 64 | tf_op jit(solution)/shard_map/psum | solution.py:74
  223.9 30.1 %psum.23 = f32[]{:T(128)} all-reduce(f32[]{:T(128)} %get-tuple-element.61), channel_id=1, replica_groups=mesh['groups'=2,'seg'=4,'blk'=4] {'seg','blk'}, use_global_device_ids=true, to_apply=%region_5.6 | all-reduce | flops 1 | bytes 8 | tf_op jit(solution)/shard_map/psum | solution.py:76
  (193 shorter events, 115.0 us)
Async XLA Ops:
  2.3 198.7 %collective-permute-start.2 = (f32[1,20,8,128]{3,2,1,0:T(8,128)}, f32[1,20,8,128]{3,2,1,0:T(8,128)}, u32[]{:S(2)}, u32[]{:S(2)}) collective-permute-start(f32[1,20,8,128]{3,2,1,0:T(8,128)} %get-tuple-element.66), channel_id=1, source_target_pairs={{4,0},{8,4},{12,8},{0,12},{5,1},{9,5},{13,9},{1,13},{6,2},{10,6},{... | collective-permute-start | bytes 245768 | tf_op jit(solution)/shard_map/ppermute | solution.py:28
  11.8 2.3 collective-permute-start
  12.6 3.3 %collective-permute-start.1 = (bf16[2,20,2,128]{3,1,2,0:T(8,128)(2,1)S(1)}, bf16[2,20,2,128]{3,1,2,0:T(8,128)(2,1)S(1)}, u32[]{:S(2)}, u32[]{:S(2)}) collective-permute-start(bf16[2,20,2,128]{3,1,2,0:T(8,128)(2,1)S(1)} %get-tuple-element.149), channel_id=1, source_target_pairs={{0,1},{1,2},{2,3},{3,0},{4,5},{5,6},{6,7},{7,4},{8,9},{9,10},{10,1... | collective-permute-start | bytes 61448 | tf_op jit(solution)/shard_map/while/body/eval_jaxpr/ppermute | solution.py:16
  23.0 1.6 collective-permute-start
  23.0 3.3 %collective-permute-start.1 = (bf16[2,20,2,128]{3,1,2,0:T(8,128)(2,1)S(1)}, bf16[2,20,2,128]{3,1,2,0:T(8,128)(2,1)S(1)}, u32[]{:S(2)}, u32[]{:S(2)}) collective-permute-start(bf16[2,20,2,128]{3,1,2,0:T(8,128)(2,1)S(1)} %get-tuple-element.149), channel_id=1, source_target_pairs={{0,1},{1,2},{2,3},{3,0},{4,5},{5,6},{6,7},{7,4},{8,9},{9,10},{10,1... | collective-permute-start | bytes 61448 | tf_op jit(solution)/shard_map/while/body/eval_jaxpr/ppermute | solution.py:16
  33.5 1.6 collective-permute-start
  33.6 3.3 %collective-permute-start.1 = (bf16[2,20,2,128]{3,1,2,0:T(8,128)(2,1)S(1)}, bf16[2,20,2,128]{3,1,2,0:T(8,128)(2,1)S(1)}, u32[]{:S(2)}, u32[]{:S(2)}) collective-permute-start(bf16[2,20,2,128]{3,1,2,0:T(8,128)(2,1)S(1)} %get-tuple-element.149), channel_id=1, source_target_pairs={{0,1},{1,2},{2,3},{3,0},{4,5},{5,6},{6,7},{7,4},{8,9},{9,10},{10,1... | collective-permute-start | bytes 61448 | tf_op jit(solution)/shard_map/while/body/eval_jaxpr/ppermute | solution.py:16
  44.1 3.3 %collective-permute-start.1 = (bf16[2,20,2,128]{3,1,2,0:T(8,128)(2,1)S(1)}, bf16[2,20,2,128]{3,1,2,0:T(8,128)(2,1)S(1)}, u32[]{:S(2)}, u32[]{:S(2)}) collective-permute-start(bf16[2,20,2,128]{3,1,2,0:T(8,128)(2,1)S(1)} %get-tuple-element.149), channel_id=1, source_target_pairs={{0,1},{1,2},{2,3},{3,0},{4,5},{5,6},{6,7},{7,4},{8,9},{9,10},{10,1... | collective-permute-start | bytes 61448 | tf_op jit(solution)/shard_map/while/body/eval_jaxpr/ppermute | solution.py:16
  54.6 3.3 %collective-permute-start.1 = (bf16[2,20,2,128]{3,1,2,0:T(8,128)(2,1)S(1)}, bf16[2,20,2,128]{3,1,2,0:T(8,128)(2,1)S(1)}, u32[]{:S(2)}, u32[]{:S(2)}) collective-permute-start(bf16[2,20,2,128]{3,1,2,0:T(8,128)(2,1)S(1)} %get-tuple-element.149), channel_id=1, source_target_pairs={{0,1},{1,2},{2,3},{3,0},{4,5},{5,6},{6,7},{7,4},{8,9},{9,10},{10,1... | collective-permute-start | bytes 61448 | tf_op jit(solution)/shard_map/while/body/eval_jaxpr/ppermute | solution.py:16
  65.2 3.3 %collective-permute-start.1 = (bf16[2,20,2,128]{3,1,2,0:T(8,128)(2,1)S(1)}, bf16[2,20,2,128]{3,1,2,0:T(8,128)(2,1)S(1)}, u32[]{:S(2)}, u32[]{:S(2)}) collective-permute-start(bf16[2,20,2,128]{3,1,2,0:T(8,128)(2,1)S(1)} %get-tuple-element.149), channel_id=1, source_target_pairs={{0,1},{1,2},{2,3},{3,0},{4,5},{5,6},{6,7},{7,4},{8,9},{9,10},{10,1... | collective-permute-start | bytes 61448 | tf_op jit(solution)/shard_map/while/body/eval_jaxpr/ppermute | solution.py:16
  75.7 3.3 %collective-permute-start.1 = (bf16[2,20,2,128]{3,1,2,0:T(8,128)(2,1)S(1)}, bf16[2,20,2,128]{3,1,2,0:T(8,128)(2,1)S(1)}, u32[]{:S(2)}, u32[]{:S(2)}) collective-permute-start(bf16[2,20,2,128]{3,1,2,0:T(8,128)(2,1)S(1)} %get-tuple-element.149), channel_id=1, source_target_pairs={{0,1},{1,2},{2,3},{3,0},{4,5},{5,6},{6,7},{7,4},{8,9},{9,10},{10,1... | collective-permute-start | bytes 61448 | tf_op jit(solution)/shard_map/while/body/eval_jaxpr/ppermute | solution.py:16
  86.2 1.6 collective-permute-start
  86.2 3.3 %collective-permute-start.1 = (bf16[2,20,2,128]{3,1,2,0:T(8,128)(2,1)S(1)}, bf16[2,20,2,128]{3,1,2,0:T(8,128)(2,1)S(1)}, u32[]{:S(2)}, u32[]{:S(2)}) collective-permute-start(bf16[2,20,2,128]{3,1,2,0:T(8,128)(2,1)S(1)} %get-tuple-element.149), channel_id=1, source_target_pairs={{0,1},{1,2},{2,3},{3,0},{4,5},{5,6},{6,7},{7,4},{8,9},{9,10},{10,1... | collective-permute-start | bytes 61448 | tf_op jit(solution)/shard_map/while/body/eval_jaxpr/ppermute | solution.py:16
  96.7 1.6 collective-permute-start
  96.8 3.3 %collective-permute-start.1 = (bf16[2,20,2,128]{3,1,2,0:T(8,128)(2,1)S(1)}, bf16[2,20,2,128]{3,1,2,0:T(8,128)(2,1)S(1)}, u32[]{:S(2)}, u32[]{:S(2)}) collective-permute-start(bf16[2,20,2,128]{3,1,2,0:T(8,128)(2,1)S(1)} %get-tuple-element.149), channel_id=1, source_target_pairs={{0,1},{1,2},{2,3},{3,0},{4,5},{5,6},{6,7},{7,4},{8,9},{9,10},{10,1... | collective-permute-start | bytes 61448 | tf_op jit(solution)/shard_map/while/body/eval_jaxpr/ppermute | solution.py:16
  107.3 3.3 %collective-permute-start.1 = (bf16[2,20,2,128]{3,1,2,0:T(8,128)(2,1)S(1)}, bf16[2,20,2,128]{3,1,2,0:T(8,128)(2,1)S(1)}, u32[]{:S(2)}, u32[]{:S(2)}) collective-permute-start(bf16[2,20,2,128]{3,1,2,0:T(8,128)(2,1)S(1)} %get-tuple-element.149), channel_id=1, source_target_pairs={{0,1},{1,2},{2,3},{3,0},{4,5},{5,6},{6,7},{7,4},{8,9},{9,10},{10,1... | collective-permute-start | bytes 61448 | tf_op jit(solution)/shard_map/while/body/eval_jaxpr/ppermute | solution.py:16
  117.8 3.3 %collective-permute-start.1 = (bf16[2,20,2,128]{3,1,2,0:T(8,128)(2,1)S(1)}, bf16[2,20,2,128]{3,1,2,0:T(8,128)(2,1)S(1)}, u32[]{:S(2)}, u32[]{:S(2)}) collective-permute-start(bf16[2,20,2,128]{3,1,2,0:T(8,128)(2,1)S(1)} %get-tuple-element.149), channel_id=1, source_target_pairs={{0,1},{1,2},{2,3},{3,0},{4,5},{5,6},{6,7},{7,4},{8,9},{9,10},{10,1... | collective-permute-start | bytes 61448 | tf_op jit(solution)/shard_map/while/body/eval_jaxpr/ppermute | solution.py:16
  128.4 3.3 %collective-permute-start.1 = (bf16[2,20,2,128]{3,1,2,0:T(8,128)(2,1)S(1)}, bf16[2,20,2,128]{3,1,2,0:T(8,128)(2,1)S(1)}, u32[]{:S(2)}, u32[]{:S(2)}) collective-permute-start(bf16[2,20,2,128]{3,1,2,0:T(8,128)(2,1)S(1)} %get-tuple-element.149), channel_id=1, source_target_pairs={{0,1},{1,2},{2,3},{3,0},{4,5},{5,6},{6,7},{7,4},{8,9},{9,10},{10,1... | collective-permute-start | bytes 61448 | tf_op jit(solution)/shard_map/while/body/eval_jaxpr/ppermute | solution.py:16
  138.9 3.3 %collective-permute-start.1 = (bf16[2,20,2,128]{3,1,2,0:T(8,128)(2,1)S(1)}, bf16[2,20,2,128]{3,1,2,0:T(8,128)(2,1)S(1)}, u32[]{:S(2)}, u32[]{:S(2)}) collective-permute-start(bf16[2,20,2,128]{3,1,2,0:T(8,128)(2,1)S(1)} %get-tuple-element.149), channel_id=1, source_target_pairs={{0,1},{1,2},{2,3},{3,0},{4,5},{5,6},{6,7},{7,4},{8,9},{9,10},{10,1... | collective-permute-start | bytes 61448 | tf_op jit(solution)/shard_map/while/body/eval_jaxpr/ppermute | solution.py:16
  149.4 3.3 %collective-permute-start.1 = (bf16[2,20,2,128]{3,1,2,0:T(8,128)(2,1)S(1)}, bf16[2,20,2,128]{3,1,2,0:T(8,128)(2,1)S(1)}, u32[]{:S(2)}, u32[]{:S(2)}) collective-permute-start(bf16[2,20,2,128]{3,1,2,0:T(8,128)(2,1)S(1)} %get-tuple-element.149), channel_id=1, source_target_pairs={{0,1},{1,2},{2,3},{3,0},{4,5},{5,6},{6,7},{7,4},{8,9},{9,10},{10,1... | collective-permute-start | bytes 61448 | tf_op jit(solution)/shard_map/while/body/eval_jaxpr/ppermute | solution.py:16
  160.0 3.3 %collective-permute-start.1 = (bf16[2,20,2,128]{3,1,2,0:T(8,128)(2,1)S(1)}, bf16[2,20,2,128]{3,1,2,0:T(8,128)(2,1)S(1)}, u32[]{:S(2)}, u32[]{:S(2)}) collective-permute-start(bf16[2,20,2,128]{3,1,2,0:T(8,128)(2,1)S(1)} %get-tuple-element.149), channel_id=1, source_target_pairs={{0,1},{1,2},{2,3},{3,0},{4,5},{5,6},{6,7},{7,4},{8,9},{9,10},{10,1... | collective-permute-start | bytes 61448 | tf_op jit(solution)/shard_map/while/body/eval_jaxpr/ppermute | solution.py:16
  170.5 3.3 %collective-permute-start.1 = (bf16[2,20,2,128]{3,1,2,0:T(8,128)(2,1)S(1)}, bf16[2,20,2,128]{3,1,2,0:T(8,128)(2,1)S(1)}, u32[]{:S(2)}, u32[]{:S(2)}) collective-permute-start(bf16[2,20,2,128]{3,1,2,0:T(8,128)(2,1)S(1)} %get-tuple-element.149), channel_id=1, source_target_pairs={{0,1},{1,2},{2,3},{3,0},{4,5},{5,6},{6,7},{7,4},{8,9},{9,10},{10,1... | collective-permute-start | bytes 61448 | tf_op jit(solution)/shard_map/while/body/eval_jaxpr/ppermute | solution.py:16
  181.1 3.3 %collective-permute-start.1 = (bf16[2,20,2,128]{3,1,2,0:T(8,128)(2,1)S(1)}, bf16[2,20,2,128]{3,1,2,0:T(8,128)(2,1)S(1)}, u32[]{:S(2)}, u32[]{:S(2)}) collective-permute-start(bf16[2,20,2,128]{3,1,2,0:T(8,128)(2,1)S(1)} %get-tuple-element.149), channel_id=1, source_target_pairs={{0,1},{1,2},{2,3},{3,0},{4,5},{5,6},{6,7},{7,4},{8,9},{9,10},{10,1... | collective-permute-start | bytes 61448 | tf_op jit(solution)/shard_map/while/body/eval_jaxpr/ppermute | solution.py:16
  191.6 3.3 %collective-permute-start.1 = (bf16[2,20,2,128]{3,1,2,0:T(8,128)(2,1)S(1)}, bf16[2,20,2,128]{3,1,2,0:T(8,128)(2,1)S(1)}, u32[]{:S(2)}, u32[]{:S(2)}) collective-permute-start(bf16[2,20,2,128]{3,1,2,0:T(8,128)(2,1)S(1)} %get-tuple-element.149), channel_id=1, source_target_pairs={{0,1},{1,2},{2,3},{3,0},{4,5},{5,6},{6,7},{7,4},{8,9},{9,10},{10,1... | collective-permute-start | bytes 61448 | tf_op jit(solution)/shard_map/while/body/eval_jaxpr/ppermute | solution.py:16
  (14 other events, 221.8 us)
